TPU v7x, 512 devices: a whole 4x8x8 slice. The times are simulated.
512 devices in a mesh: ctx: 64 (over y, z), kv: 8 (over x, core).
Axes of the slice: x: 4, y: 8, z: 8, core: 2. Of those that a mesh axis runs over, the one named last changes fastest.
Arguments:
- queries: bfloat16 [16384, 64, 128], P(('ctx', 'kv')), may hold values from -150 to 150
- keys: bfloat16 [16384, 8, 128], P(('ctx', 'kv')), may hold values from -5 to 5
- values: bfloat16 [16384, 8, 128], P(('ctx', 'kv')), may hold values from -6 to 6
- doc_ids: int32 [16384], P('ctx'), may hold values from 0 to 15, never falling along the last dimension, each value on 1 to 8448 neighbouring positions
Outputs:
- attended: bfloat16 [16384, 64, 128], P(('ctx', 'kv'))
Inputs may be any that keep to these rules, and one draw needn't show every extreme that they name: `doc_ids`: document numbers never fall along the sequence; each document holds 1 to 8448 tokens, and one holds exactly 8448.
All inputs are finite; a program needn't handle non-finite values.
Results may differ from a plain program's by a relative error of at most 0.0055.
Values may be sent and summed in bfloat16 or wider, within the bound.
A program may use at most 64 MiB of HBM per device.

v0:
```python
import math

import jax
import jax.numpy as jnp
from jax import lax
from jax.experimental import pallas as pl
from jax.experimental.pallas import tpu as pltpu
from jax.sharding import PartitionSpec as P

ROWS, COLS, XS, CS = 8, 8, 4, 2
TOK, HD, PG = 32, 128, 8
QROWS = TOK * PG
BLK = XS * CS * TOK
ROWTOK = COLS * BLK
BIG = 1e30
C = math.log2(math.e) / math.sqrt(HD)
MESH = pl.DeviceIdType.MESH
F32, BF16 = jnp.float32, jnp.bfloat16
NT = (((1,), (1,)), ((), ()))
NN = (((1,), (0,)), ((), ()))


def wide(x, k):
    return jnp.concatenate([x] * k, axis=1)


def kernel(
    qs, kvs, cnt, o_ref,
    qbuf, kvbuf, qa, kaug, acc, top, sbuf, obuf, cy, cz,
    loc, kva_s, kva_r, q_s, q_r, cy_s, cy_r, cz_s, cz_r, o_s, o_r,
    x0_s, x0_r, vz_s, vz_r, kz_s, kz_r, vx_s, vx_r, sib_s, sib_r,
):
    ctx, kv = lax.axis_index("ctx"), lax.axis_index("kv")
    y, z, x, c = ctx // COLS, ctx % COLS, kv // CS, kv % CS

    def on_y(d):
        return (((y + d) % ROWS) * COLS + z, kv)

    def on_z(d):
        return (y * COLS + (z + d) % COLS, kv)

    def on_x(d):
        return (ctx, ((x + d) % XS) * CS + c)

    sibling = (ctx, x * CS + 1 - c)

    def remote(src, dst, ss, rs, dev):
        return pltpu.make_async_remote_copy(
            src_ref=src, dst_ref=dst, send_sem=ss, recv_sem=rs, device_id=dev, device_id_type=MESH
        )

    def kva(d):
        return remote(kvs.at[(y + d) % ROWS], kvbuf.at[:, y, z, x, c], kva_s.at[d], kva_r.at[d], on_y(d))

    def qcopy(d):
        return remote(qs.at[(y + d) % ROWS], qbuf.at[y], q_s.at[d], q_r.at[d], on_y(d))

    def cycopy(d):
        return remote(cnt, cy.at[y], cy_s.at[d], cy_r.at[d], on_y(d))

    def czcopy(d):
        return remote(cz.at[z], cz.at[z], cz_s.at[d], cz_r.at[d], on_z(d))

    def x0(d):
        at = kvbuf.at[:, :, z, x, c]
        return remote(at, at, x0_s.at[d], x0_r.at[d], on_x(d))

    def rows_of(half):
        return pl.ds(0, ROWS) if half is None else pl.ds(half * (ROWS // 2), ROWS // 2)

    def vz(way, hop, half=None):
        zz = (z + (COLS + 1 - hop if way == 0 else hop - 1)) % COLS
        at = kvbuf.at[1, rows_of(half), zz, x, c]
        return remote(at, at, vz_s.at[way, hop], vz_r.at[way, hop], on_z(1 if way == 0 else COLS - 1))

    def kz(way, hop, half=None):
        zz = (z + (COLS + 1 - hop if way == 0 else hop - 1)) % COLS
        at = kvbuf.at[0, rows_of(half), zz, :, c]
        return remote(at, at, kz_s.at[way, hop], kz_r.at[way, hop], on_z(1 if way == 0 else COLS - 1))

    def vx(off, d):
        at = kvbuf.at[1, :, (z + off) % COLS, x, c]
        return remote(at, at, vx_s.at[off, d], vx_r.at[off, d], on_x(d))

    def sib(off):
        at = kvbuf.at[:, :, (z + off) % COLS, :, c]
        return remote(at, at, sib_s.at[off], sib_r.at[off], sibling)

    def ocopy(d):
        return remote(obuf.at[(y + d) % ROWS], o_ref.at[y], o_s.at[d], o_r.at[d], on_y(d))

    barrier = pltpu.get_barrier_semaphore()
    peers = [on_y(d) for d in range(1, ROWS)] + [on_z(d) for d in range(1, COLS)]
    peers += [on_x(d) for d in range(1, XS)] + [sibling]
    for dev in peers:
        pl.semaphore_signal(barrier, inc=1, device_id=dev, device_id_type=MESH)
    pl.semaphore_wait(barrier, len(peers))

    order = (1, 7, 2, 6, 3, 5, 4)
    for d in order:
        kva(d).start()
    for d in order:
        cycopy(d).start()
    own_kv = pltpu.make_async_copy(kvs.at[y], kvbuf.at[:, y, z, x, c], loc.at[0])
    own_q = pltpu.make_async_copy(qs.at[y], qbuf.at[y], loc.at[1])
    own_kv.start()
    own_q.start()
    for d in order:
        qcopy(d).start()
    for d in order:
        kva(d).wait_recv()
    own_kv.wait()

    vz(0, 1).start()
    vz(1, 1).start()
    for d in (1, 3, 2):
        x0(d).start()
    for d in order:
        cycopy(d).wait_recv()
    cy[y] = cnt[...]
    line = cy[0]
    for r in range(1, ROWS):
        line = line + cy[r]
    cz[z] = line
    for d in order:
        czcopy(d).start()

    def v_step(hop):
        vz(0, hop).wait_recv()
        vz(1, hop).wait_recv()
        if hop < 3:
            vz(0, hop + 1).start()
            vz(1, hop + 1).start()
        else:
            vz(0, 4, 0).start()
            vz(1, 4, 1).start()
        for off in (COLS - hop, hop):
            for d in (1, 3, 2):
                vx(off, d).start()

    v_step(1)
    for d in (1, 3, 2):
        x0(d).wait_recv()
    kz(0, 1).start()
    kz(1, 1).start()
    sib(0).start()
    v_step(2)

    for d in order:
        czcopy(d).wait_recv()
    total = cz[0]
    for r in range(1, COLS):
        total = total + cz[r]
    first, last = total[0:1], total[4:5]
    lane = lax.broadcasted_iota(jnp.int32, (1, HD), 1)
    sign = jnp.where(lane < 16, 1, -1)
    row256 = lax.broadcasted_iota(jnp.int32, (BLK, HD), 0)
    here = BLK * z + (CS * TOK) * x + TOK * c

    @pl.loop(0, ROWS)
    def _(r):
        pos = ROWTOK * r + here + row256 // PG
        same = (pos >= first) & (pos < last) & (lane < 16)
        qa[r] = jnp.where(same | (lane == 16 + r), -BIG, 0.0).astype(BF16)

    @pl.loop(0, COLS)
    def _(zk):
        bound = ROWTOK * (lane - 16 + jnp.where(zk < z, 1, 0))
        limit = jnp.where(lane < 16, first, 1 - bound)

        @pl.loop(0, ROWS)
        def _(r):
            pos = ROWTOK * r + BLK * zk + row256
            kaug[zk, r] = jnp.where(pos * sign < limit, 1.0, 0.0).astype(BF16)

    v_step(3)
    vz(0, 4, 0).wait_recv()
    vz(1, 4, 1).wait_recv()
    for d in (1, 3, 2):
        vx(4, d).start()
    for d in order:
        qcopy(d).wait_recv()
    own_q.wait()
    sib(0).wait_recv()

    def s_tile(r, r0, zk):
        q = jnp.concatenate([qbuf[r], qa[r]], axis=1)
        k = kvbuf[0, pl.ds(r0, 2), zk].reshape(2 * BLK, HD)
        k = jnp.concatenate([k, kaug[zk, pl.ds(r0, 2)].reshape(2 * BLK, HD)], axis=1)
        return lax.dot_general(q, k, NT, preferred_element_type=F32)

    def top_of(s):
        mx = s[:, :HD]
        for j in range(1, s.shape[1] // HD):
            mx = jnp.maximum(mx, s[:, j * HD:(j + 1) * HD])
        return jnp.max(mx, axis=1, keepdims=True)

    def weigh(s, mn, v):
        p = jnp.exp2((s - wide(mn, s.shape[1] // HD)) * C).astype(BF16)
        v = jnp.concatenate([v, jnp.ones_like(v)], axis=1)
        return lax.dot_general(p, v, NN, preferred_element_type=F32)

    def update(r, r0, zk, s):
        old = top[r]
        new = jnp.maximum(old, top_of(s))
        fade = jnp.exp2((old - new) * C)
        top[r] = new
        v = kvbuf[1, pl.ds(r0, 2), zk].reshape(2 * BLK, HD)
        acc[r] = acc[r] * wide(fade, 2) + weigh(s, new, v)

    @pl.loop(0, ROWS)
    def _(r):
        q = jnp.concatenate([qbuf[r], jnp.where(lane < 16, qa[r], 0.0).astype(BF16)], axis=1)
        k = jnp.concatenate([kvbuf[0, r, z].reshape(BLK, HD), kaug[z, r]], axis=1)
        s = lax.dot_general(q, k, NT, preferred_element_type=F32)
        at = (CS * TOK) * x + TOK * c + lax.broadcasted_iota(jnp.int32, (QROWS, BLK), 0) // PG
        s = jnp.where(lax.broadcasted_iota(jnp.int32, (QROWS, BLK), 1) <= at, s, -BIG)
        new = jnp.broadcast_to(top_of(s), (QROWS, HD))
        top[r] = new
        acc[r] = weigh(s, new, kvbuf[1, r, z].reshape(BLK, HD))

    def run(place, tiles, unroll):
        sbuf[0] = s_tile(*place(0))

        @pl.loop(0, tiles // unroll)
        def _(i):
            for u in range(unroll):
                f = i * unroll + u
                sbuf[(u + 1) % 2] = s_tile(*place(jnp.minimum(f + 1, tiles - 1)))
                update(*place(f), sbuf[u % 2])

    def base(r, zk, spread):
        high = r - jnp.where(zk < z, 0, 1)
        return jnp.maximum(high - spread, 0)

    def most(zk):
        def place(f):
            r = jnp.where(f < 2, f, 2 + (f - 2) // 2)
            r0 = base(r, zk, 3) + jnp.where(f < 2, 0, 2 * (f % 2))
            return r, r0, zk
        return place

    @pl.loop(1, 4)
    def _(k):
        for way in range(2):
            kz(way, k).wait_recv()

        @pl.when(k < 3)
        def _():
            for way in range(2):
                kz(way, k + 1).start()

        @pl.when(k == 3)
        def _():
            for way in range(2):
                kz(way, 4, way).start()

        for off in (COLS - k, k):
            for d in (1, 3, 2):
                vx(off, d).wait_recv()
            sib(off).start()

        @pl.loop(0, 2)
        def _(j):
            @pl.when(j == 1)
            def _():
                sib(COLS - k).wait_recv()

            zk = (z + jnp.where(j == 0, k - 1, COLS - k)) % COLS
            run(most(zk), 14, 14)

        sib(k).wait_recv()

    kz(0, 4, 0).wait_recv()
    kz(1, 4, 1).wait_recv()
    for d in (1, 3, 2):
        vx(4, d).wait_recv()
    sib(4).start()

    before = (z + COLS - 1) % COLS

    @pl.loop(4, ROWS)
    def _(r):
        row = r - 4 - jnp.where(before < z, 0, 1)

        @pl.when(row >= 0)
        def _():
            q = jnp.concatenate([qbuf[r], qa[r]], axis=1)
            k = jnp.concatenate([kvbuf[0, row, before].reshape(BLK, HD), kaug[before, row]], axis=1)
            s = lax.dot_general(q, k, NT, preferred_element_type=F32)
            old = top[r]
            new = jnp.maximum(old, top_of(s))
            top[r] = new
            v = kvbuf[1, row, before].reshape(BLK, HD)
            acc[r] = acc[r] * wide(jnp.exp2((old - new) * C), 2) + weigh(s, new, v)

    sib(4).wait_recv()

    def dist(i):
        return 4 + ((i + 1) // 2) * (1 - 2 * (i % 2))

    def last_place(f):
        r = (y + dist(f // 4)) % ROWS
        zk = (z + 3 + (f % 4) // 2) % COLS
        return r, base(r, zk, 3) + 2 * (f % 2), zk

    sbuf[0] = s_tile(*last_place(0))

    @pl.loop(0, ROWS)
    def _(i):
        d = dist(i)
        r = (y + d) % ROWS
        for u in range(4):
            f = 4 * i + u
            sbuf[(u + 1) % 2] = s_tile(*last_place(jnp.minimum(f + 1, 4 * ROWS - 1)))
            update(*last_place(f), sbuf[u % 2])
        done = acc[r]
        obuf[r] = (done[:, :HD] / done[:, HD:]).astype(BF16)

        @pl.when(d > 0)
        def _():
            ocopy(d).start()

    own_o = pltpu.make_async_copy(obuf.at[y], o_ref.at[y], loc.at[2])
    own_o.start()

    for d in order:
        kva(d).wait_send()
        qcopy(d).wait_send()
        cycopy(d).wait_send()
        czcopy(d).wait_send()
    for way in range(2):
        for hop in (1, 2, 3):
            vz(way, hop).wait_send()
            kz(way, hop).wait_send()
        vz(way, 4, way).wait_send()
        kz(way, 4, way).wait_send()
    for d in range(1, XS):
        x0(d).wait_send()
        for off in range(1, COLS):
            vx(off, d).wait_send()
    for off in range(COLS):
        sib(off).wait_send()
    own_o.wait()
    for d in order:
        ocopy(d).wait()


def attend(queries, keys, values, doc_ids):
    qs = queries.reshape(TOK, ROWS, PG, HD).transpose(1, 0, 2, 3).reshape(ROWS, QROWS, HD)
    kvs = jnp.stack([keys, values]).transpose(2, 0, 1, 3)
    docs = jnp.arange(HD, dtype=jnp.int32)
    below = jnp.sum((doc_ids[:, None] < docs[None, :]).astype(jnp.int32), axis=0)
    upto = jnp.sum((doc_ids[:, None] <= docs[None, :]).astype(jnp.int32), axis=0)
    cnt = jnp.repeat(jnp.stack([below, upto]), 4, axis=0)
    dma = pltpu.SemaphoreType.DMA
    vmem = pl.BlockSpec(memory_space=pltpu.VMEM)
    out = pl.pallas_call(
        kernel,
        out_shape=jax.ShapeDtypeStruct((ROWS, QROWS, HD), BF16),
        in_specs=[vmem, vmem, vmem],
        out_specs=pl.BlockSpec(memory_space=pl.ANY),
        scratch_shapes=[
            pltpu.VMEM((ROWS, QROWS, HD), BF16),
            pltpu.VMEM((2, ROWS, COLS, XS, CS, TOK, HD), BF16),
            pltpu.VMEM((ROWS, QROWS, HD), BF16),
            pltpu.VMEM((COLS, ROWS, BLK, HD), BF16),
            pltpu.VMEM((ROWS, QROWS, 2 * HD), F32),
            pltpu.VMEM((ROWS, QROWS, HD), F32),
            pltpu.VMEM((2, QROWS, 2 * BLK), F32),
            pltpu.VMEM((ROWS, QROWS, HD), BF16),
            pltpu.VMEM((ROWS, 8, HD), jnp.int32),
            pltpu.VMEM((COLS, 8, HD), jnp.int32),
            dma((3,)),
            *[dma((8,))] * 10,
            *[dma((4,))] * 2,
            *[dma((2, 5))] * 4,
            *[dma((8, 4))] * 2,
            *[dma((8,))] * 2,
        ],
        compiler_params=pltpu.CompilerParams(
            collective_id=0, has_side_effects=True, vmem_limit_bytes=50 * 2**20
        ),
        name="attend",
    )(qs, kvs, cnt)
    return out.reshape(ROWS, TOK, PG, HD).transpose(1, 0, 2, 3).reshape(TOK, ROWS * PG, HD)


def solution(mesh):
    tokens = P(("ctx", "kv"), None, None)
    return jax.shard_map(
        attend,
        mesh=mesh,
        in_specs=(tokens, tokens, tokens, P("ctx")),
        out_specs=tokens,
        check_vma=False,
    )
```

profile of v0, /device:TPU:1, one launch (start us, length us, event | category | flops | bytes accessed | tf_op | source)
XLA Modules:
  0.0 85.8 jit_solution(7411940071072995239)
XLA Ops:
  0.0 0.0 copy-start
  0.0 0.8 convert_reduce_fusion.1
  0.9 0.9 %copy_bitcast_fusion.2 = (bf16[1,32,8,128]{3,1,0,2:T(8,128)(2,1)S(1)}, bf16[1,32,8,128]{3,1,0,2:T(8,128)(2,1)S(1)}) fusion(bf16[32,8,128]{2,1,0:T(8,128)(2,1)} %param.6, bf16[32,8,128]{2,1,0:T(8,128)(2,1)} %param.5), kind=kLoop, calls=%fused_computation.7 | loop fusion | bytes 262144 | tf_op jit(solution)/shard_map/stack | solution.py:351
  1.8 0.0 copy-done
  1.8 0.1 copy_bitcast_fusion.1.qs
  1.9 82.9 %attend.1 = bf16[8,256,128]{2,1,0:T(8,128)(2,1)S(1)} custom-call(bf16[8,256,128]{2,1,0:T(8,128)(2,1)S(1)} %copy_bitcast_fusion.1.qs, bf16[8,2,32,128]{3,2,1,0:T(8,128)(2,1)S(1)} %maximum_bitcast_fusion.kvs, s32[8,128]{1,0:T(8,128)S(1)} %bitcast.23), custom_call_target="tpu_custom_call" | custom-call | tf_op jit(solution)/shard_map/attend/pallas_call | solution.py:358
  84.8 0.9 %copy_bitcast_fusion = bf16[32,64,128]{2,1,0:T(8,128)(2,1)} fusion(bf16[8,256,128]{2,1,0:T(8,128)(2,1)S(1)} %attend.1), kind=kLoop, calls=%fused_computation | loop fusion | bytes 1048576 | tf_op jit(solution)/shard_map/reshape | solution.py:386
  (3 shorter events, 0.0 us)
Async XLA Ops:
  0.0 1.8 %copy-start = (bf16[32,64,128]{2,1,0:T(8,128)(2,1)S(1)}, bf16[32,64,128]{2,1,0:T(8,128)(2,1)}, u32[]{:S(2)}) copy-start(bf16[32,64,128]{2,1,0:T(8,128)(2,1)} %param.4) | copy-start | bytes 1572868
where the time goes:
time: 85.9 us; the launch traced here: 85.8 us
  Pallas kernels  82.9 us (97%)
  local copies, waits for them, and re-layouts  1.93 us (2%)
  other arithmetic  0.88 us (1%)
    pallas_call x1, Pallas kernels, attend(): pl.pallas_call(kernel, out_shape=jax.ShapeDtypeStruct((ROWS, QROWS, HD),...  82.9 us

commit v1 on v0

v1 whole, which is shorter than its diff:
```python
import math

import jax
import jax.numpy as jnp
from jax import lax
from jax.experimental import pallas as pl
from jax.experimental.pallas import tpu as pltpu
from jax.sharding import PartitionSpec as P

ROWS, COLS, XS, CS = 8, 8, 4, 2
TOK, HD, PG = 32, 128, 8
QROWS = TOK * PG
BLK = XS * CS * TOK
ROWTOK = COLS * BLK
DOCS = 16
BIG = 1e30
C = math.log2(math.e) / math.sqrt(HD)
MESH = pl.DeviceIdType.MESH
F32, BF16 = jnp.float32, jnp.bfloat16
NT = (((1,), (1,)), ((), ()))
NN = (((1,), (0,)), ((), ()))


LATE = (3, 4, 5)


def wide(x, k):
    return jnp.concatenate([x] * k, axis=1)


def kernel(
    qs, kvs, ids, o_ref,
    qbuf, kvbuf, qa, kaug, acc, top, sbuf, obuf, cy, cz,
    loc, kva_s, kva_r, q_s, q_r, cy_s, cy_r, cz_s, cz_r, o_s, o_r,
    x0_s, x0_r, vz_s, vz_r, kz_s, kz_r, vx_s, vx_r, sib_s, sib_r,
):
    ctx, kv = lax.axis_index("ctx"), lax.axis_index("kv")
    y, z, x, c = ctx // COLS, ctx % COLS, kv // CS, kv % CS

    def on_y(d):
        return (((y + d) % ROWS) * COLS + z, kv)

    def on_z(d):
        return (y * COLS + (z + d) % COLS, kv)

    def on_x(d):
        return (ctx, ((x + d) % XS) * CS + c)

    sibling = (ctx, x * CS + 1 - c)

    def remote(src, dst, ss, rs, dev):
        return pltpu.make_async_remote_copy(
            src_ref=src, dst_ref=dst, send_sem=ss, recv_sem=rs, device_id=dev, device_id_type=MESH
        )

    def kva(d):
        return remote(kvs.at[(y + d) % ROWS], kvbuf.at[:, y, z, x, c], kva_s.at[d], kva_r.at[d], on_y(d))

    def qcopy(d):
        return remote(qs.at[(y + d) % ROWS], qbuf.at[y], q_s.at[d], q_r.at[d], on_y(d))

    def cycopy(d):
        return remote(cy.at[y], cy.at[y], cy_s.at[d], cy_r.at[d], on_y(d))

    def czcopy(d):
        return remote(cz.at[z], cz.at[z], cz_s.at[d], cz_r.at[d], on_z(d))

    def x0(which, d):
        at = kvbuf.at[which, :, z, x, c]
        return remote(at, at, x0_s.at[which, d], x0_r.at[which, d], on_x(d))

    def rows_of(half):
        return pl.ds(0, ROWS) if half is None else pl.ds(half * (ROWS // 2), ROWS // 2)

    def column(way, hop):
        return (z + (COLS + 1 - hop if way == 0 else hop - 1)) % COLS

    def vz(way, hop, half=None):
        at = kvbuf.at[1, rows_of(half), column(way, hop), x, c]
        return remote(at, at, vz_s.at[way, hop], vz_r.at[way, hop], on_z(1 if way == 0 else COLS - 1))

    def kz(way, hop, piece):
        at = kvbuf.at[0, :, column(way, hop), (x + (0, 3, 1, 2)[piece]) % XS, c]
        return remote(
            at, at, kz_s.at[way, hop, piece], kz_r.at[way, hop, piece], on_z(1 if way == 0 else COLS - 1)
        )

    def vx(off, d):
        at = kvbuf.at[1, :, (z + off) % COLS, x, c]
        return remote(at, at, vx_s.at[off, d], vx_r.at[off, d], on_x(d))

    def sib(off):
        at = kvbuf.at[:, :, (z + off) % COLS, :, c]
        return remote(at, at, sib_s.at[off], sib_r.at[off], sibling)

    def ocopy(d):
        return remote(obuf.at[(y + d) % ROWS], o_ref.at[y], o_s.at[d], o_r.at[d], on_y(d))

    barrier = pltpu.get_barrier_semaphore()
    peers = [on_y(d) for d in range(1, ROWS)] + [on_z(d) for d in range(1, COLS)]
    peers += [on_x(d) for d in range(1, XS)] + [sibling]
    for dev in peers:
        pl.semaphore_signal(barrier, inc=1, device_id=dev, device_id_type=MESH)

    lane = lax.broadcasted_iota(jnp.int32, (1, HD), 1)
    below = jnp.where(lane == 0, 0, BLK)
    upto = jnp.full((1, HD), BLK, jnp.int32)
    for d in range(1, DOCS):
        count = jnp.sum(jnp.where(ids[...] < d, 1.0, 0.0), axis=1, keepdims=True)
        count = jnp.sum(count, axis=0, keepdims=True).astype(jnp.int32)
        below = jnp.where(lane == d, count, below)
        upto = jnp.where(lane == d - 1, count, upto)
    row8 = lax.broadcasted_iota(jnp.int32, (8, HD), 0)
    cy[y] = jnp.where(row8 < 4, below, upto)

    pl.semaphore_wait(barrier, len(peers))

    order = (1, 7, 2, 6, 3, 5, 4)
    near = (1, 3, 2)
    ways = (0, 1)
    for d in order:
        kva(d).start()
    for d in order:
        cycopy(d).start()
    own_kv = pltpu.make_async_copy(kvs.at[y], kvbuf.at[:, y, z, x, c], loc.at[0])
    own_q = pltpu.make_async_copy(qs.at[y], qbuf.at[y], loc.at[1])
    own_kv.start()
    own_q.start()
    for d in order:
        qcopy(d).start()
    for d in order:
        kva(d).wait_recv()
    own_kv.wait()

    for way in ways:
        vz(way, 1).start()
    for d in near:
        x0(0, d).start()
    for way in ways:
        kz(way, 1, 0).start()
    for d in near:
        x0(1, d).start()
    for d in order:
        cycopy(d).wait_recv()
    line = cy[0]
    for r in range(1, ROWS):
        line = line + cy[r]
    cz[z] = line
    for d in order:
        czcopy(d).start()
    for piece in (1, 2, 3):
        x0(0, near[piece - 1]).wait_recv()
        for way in ways:
            kz(way, 1, piece).start()

    def v_event(hop):
        for way in ways:
            if hop < 4:
                vz(way, hop).wait_recv()
            else:
                vz(way, 4, way).wait_recv()
            if hop < 3:
                vz(way, hop + 1).start()
            elif hop == 3:
                vz(way, 4, way).start()
        for off in (COLS - hop, hop) if hop < 4 else (4,):
            for d in near:
                vx(off, d).start()

    def k_event(hop, pieces):
        mine = 0 if pieces[0] == 0 else 1
        for piece in pieces:
            for way in ways:
                if hop < 4 or way == mine:
                    kz(way, hop, piece).wait_recv()
                if hop < 3 or (hop == 3 and way == mine):
                    kz(way, hop + 1, piece).start()

    def pass_on(off):
        for d in near:
            vx(off, d).wait_recv()
        sib(off).start()

    v_event(1)
    for d in order:
        czcopy(d).wait_recv()
    total = cz[0]
    for r in range(1, COLS):
        total = total + cz[r]
    first, last = total[0:1], total[4:5]
    sign = jnp.where(lane < DOCS, 1, -1)
    row256 = lax.broadcasted_iota(jnp.int32, (BLK, HD), 0)
    here = BLK * z + (CS * TOK) * x + TOK * c

    @pl.loop(0, ROWS)
    def _(r):
        pos = ROWTOK * r + here + row256 // PG
        same = (pos >= first) & (pos < last) & (lane < DOCS)
        qa[r] = jnp.where(same | (lane == DOCS + r), -BIG, 0.0).astype(BF16)

    @pl.loop(0, COLS)
    def _(zk):
        bound = ROWTOK * (lane - DOCS + jnp.where(zk < z, 1, 0))
        limit = jnp.where(lane < DOCS, first, 1 - bound)

        @pl.loop(0, ROWS)
        def _(r):
            pos = ROWTOK * r + BLK * zk + row256
            kaug[zk, r] = jnp.where(pos * sign < limit, 1.0, 0.0).astype(BF16)

    k_event(1, (0, 1))
    for d in near:
        x0(1, d).wait_recv()
    sib(0).start()

    v_event(2)
    sib(0).wait_recv()

    def s_tile(r, r0, zk):
        q = jnp.concatenate([qbuf[r], qa[r]], axis=1)
        k = kvbuf[0, pl.ds(r0, 2), zk].reshape(2 * BLK, HD)
        k = jnp.concatenate([k, kaug[zk, pl.ds(r0, 2)].reshape(2 * BLK, HD)], axis=1)
        return lax.dot_general(q, k, NT, preferred_element_type=F32)

    def v_tile(r0, zk):
        return kvbuf[1, pl.ds(r0, 2), zk].reshape(2 * BLK, HD)

    def top_of(s):
        mx = s[:, :HD]
        for j in range(1, s.shape[1] // HD):
            mx = jnp.maximum(mx, s[:, j * HD:(j + 1) * HD])
        return jnp.max(mx, axis=1, keepdims=True)

    def weigh(s, mn, v):
        p = jnp.exp2((s - wide(mn, s.shape[1] // HD)) * C).astype(BF16)
        v = jnp.concatenate([v, jnp.ones_like(v)], axis=1)
        return lax.dot_general(p, v, NN, preferred_element_type=F32)

    def update(r, r0, zk, s):
        old = top[r]
        new = jnp.maximum(old, top_of(s))
        fade = jnp.exp2((old - new) * C)
        top[r] = new
        acc[r] = acc[r] * wide(fade, 2) + weigh(s, new, v_tile(r0, zk))

    def base(r, zk, spread):
        high = r - jnp.where(zk < z, 0, 1)
        return jnp.maximum(high - spread, 0)

    @pl.loop(0, ROWS)
    def _(i):
        half = (i + 1) // 2
        d = (half + (i + 1) % 2 * (COLS - 2 * half)) % ROWS

        @pl.when(i == 0)
        def _():
            own_q.wait()

        @pl.when(i > 0)
        def _():
            qcopy(d).wait_recv()

        r = (y + ROWS - d) % ROWS
        r0 = base(r, z, 3)
        q = jnp.concatenate([qbuf[r], jnp.where(lane < DOCS, qa[r], 0.0).astype(BF16)], axis=1)
        k = jnp.concatenate([kvbuf[0, r, z].reshape(BLK, HD), kaug[z, r]], axis=1)
        s = lax.dot_general(q, k, NT, preferred_element_type=F32)
        at = (CS * TOK) * x + TOK * c + lax.broadcasted_iota(jnp.int32, (QROWS, BLK), 0) // PG
        s = jnp.where(lax.broadcasted_iota(jnp.int32, (QROWS, BLK), 1) <= at, s, -BIG)
        s1, s2 = s_tile(r, r0, z), s_tile(r, r0 + 2, z)
        new = jnp.maximum(jnp.maximum(top_of(s), top_of(s1)), top_of(s2))
        new = jnp.broadcast_to(new, (QROWS, HD))
        top[r] = new
        acc[r] = (
            weigh(s, new, kvbuf[1, r, z].reshape(BLK, HD))
            + weigh(s1, new, v_tile(r0, z))
            + weigh(s2, new, v_tile(r0 + 2, z))
        )

        @pl.when(i == 1)
        def _():
            k_event(1, (2, 3))

        @pl.when(i == 3)
        def _():
            v_event(3)

        @pl.when(i == 5)
        def _():
            pass_on(7)

    pass_on(1)
    k_event(2, (0, 1))

    def run(place, tiles):
        sbuf[0] = s_tile(*place(0))
        for f in range(tiles):
            if f + 1 < tiles:
                sbuf[(f + 1) % 2] = s_tile(*place(f + 1))
            update(*place(f), sbuf[f % 2])

    @pl.loop(0, 4)
    def _(g):
        off = jnp.where(g % 2 == 0, COLS - 1 - g // 2, 1 + g // 2)
        zk = (z + off) % COLS
        sib(off).wait_recv()

        def place(f):
            r = f if f < 2 else 2 + (f - 2) // 2
            return r, base(r, zk, 3) + (0 if f < 2 else 2 * (f % 2)), zk

        run(place, 14)

        @pl.when(g == 0)
        def _():
            k_event(2, (2, 3))
            v_event(4)
            pass_on(6)

        @pl.when(g == 1)
        def _():
            k_event(3, (0, 1))
            pass_on(2)

        @pl.when(g == 2)
        def _():
            k_event(3, (2, 3))
            pass_on(5)

        @pl.when(g == 3)
        def _():
            k_event(4, (0, 1))
            k_event(4, (2, 3))
            pass_on(3)
            pass_on(4)

    before = (z + COLS - 1) % COLS

    @pl.loop(4, ROWS)
    def _(r):
        row = r - 4 - jnp.where(before < z, 0, 1)

        @pl.when(row >= 0)
        def _():
            q = jnp.concatenate([qbuf[r], qa[r]], axis=1)
            k = jnp.concatenate([kvbuf[0, row, before].reshape(BLK, HD), kaug[before, row]], axis=1)
            s = lax.dot_general(q, k, NT, preferred_element_type=F32)
            old = top[r]
            new = jnp.maximum(old, top_of(s))
            top[r] = new
            v = kvbuf[1, row, before].reshape(BLK, HD)
            acc[r] = acc[r] * wide(jnp.exp2((old - new) * C), 2) + weigh(s, new, v)

    for off in LATE:
        sib(off).wait_recv()

    def dist(i):
        return 4 + ((i + 1) // 2) * (1 - 2 * (i % 2))

    def last_place(f):
        r = (y + dist(f // (2 * len(LATE)))) % ROWS
        zk = (z + LATE[0] + (f // 2) % len(LATE)) % COLS
        return r, base(r, zk, 3) + 2 * (f % 2), zk

    sbuf[0] = s_tile(*last_place(0))

    @pl.loop(0, ROWS)
    def _(i):
        d = dist(i)
        r = (y + d) % ROWS
        for u in range(2 * len(LATE)):
            f = 2 * len(LATE) * i + u
            sbuf[(u + 1) % 2] = s_tile(*last_place(jnp.minimum(f + 1, 2 * len(LATE) * ROWS - 1)))
            update(*last_place(f), sbuf[u % 2])
        done = acc[r]
        obuf[r] = (done[:, :HD] / done[:, HD:]).astype(BF16)

        @pl.when(d > 0)
        def _():
            ocopy(d).start()

    own_o = pltpu.make_async_copy(obuf.at[y], o_ref.at[y], loc.at[2])
    own_o.start()

    for d in order:
        kva(d).wait_send()
        qcopy(d).wait_send()
        cycopy(d).wait_send()
        czcopy(d).wait_send()
    for way in ways:
        for hop in (1, 2, 3):
            vz(way, hop).wait_send()
            for piece in range(4):
                kz(way, hop, piece).wait_send()
        vz(way, 4, way).wait_send()
        for piece in (2 * way, 2 * way + 1):
            kz(way, 4, piece).wait_send()
    for d in near:
        x0(0, d).wait_send()
        x0(1, d).wait_send()
        for off in range(1, COLS):
            vx(off, d).wait_send()
    for off in range(COLS):
        sib(off).wait_send()
    own_o.wait()
    for d in order:
        ocopy(d).wait()


def attend(queries, keys, values, doc_ids):
    qs = queries.reshape(TOK, ROWS, PG, HD).transpose(1, 0, 2, 3).reshape(ROWS, QROWS, HD)
    kvs = jnp.stack([keys, values]).transpose(2, 0, 1, 3)
    dma = pltpu.SemaphoreType.DMA
    vmem = pl.BlockSpec(memory_space=pltpu.VMEM)
    out = pl.pallas_call(
        kernel,
        out_shape=jax.ShapeDtypeStruct((ROWS, QROWS, HD), BF16),
        in_specs=[vmem, vmem, vmem],
        out_specs=pl.BlockSpec(memory_space=pl.ANY),
        scratch_shapes=[
            pltpu.VMEM((ROWS, QROWS, HD), BF16),
            pltpu.VMEM((2, ROWS, COLS, XS, CS, TOK, HD), BF16),
            pltpu.VMEM((ROWS, QROWS, HD), BF16),
            pltpu.VMEM((COLS, ROWS, BLK, HD), BF16),
            pltpu.VMEM((ROWS, QROWS, 2 * HD), F32),
            pltpu.VMEM((ROWS, QROWS, HD), F32),
            pltpu.VMEM((2, QROWS, 2 * BLK), F32),
            pltpu.VMEM((ROWS, QROWS, HD), BF16),
            pltpu.VMEM((ROWS, 8, HD), jnp.int32),
            pltpu.VMEM((COLS, 8, HD), jnp.int32),
            dma((3,)),
            *[dma((8,))] * 10,
            *[dma((2, 4))] * 2,
            *[dma((2, 5))] * 2,
            *[dma((2, 5, 4))] * 2,
            *[dma((8, 4))] * 2,
            *[dma((8,))] * 2,
        ],
        compiler_params=pltpu.CompilerParams(
            collective_id=0, has_side_effects=True, vmem_limit_bytes=50 * 2**20
        ),
        name="attend",
    )(qs, kvs, doc_ids.reshape(2, HD))
    return out.reshape(ROWS, TOK, PG, HD).transpose(1, 0, 2, 3).reshape(TOK, ROWS * PG, HD)


def solution(mesh):
    tokens = P(("ctx", "kv"), None, None)
    return jax.shard_map(
        attend,
        mesh=mesh,
        in_specs=(tokens, tokens, tokens, P("ctx")),
        out_specs=tokens,
        check_vma=False,
    )
```

time: 85.9 us -> 77.7 us (0.905)
  Pallas kernels: 82.9 us -> 74.9 us
  other arithmetic: 0.88 us -> 0.02 us
    pallas_call x1, Pallas kernels: 82.9 us -> 74.9 us  [attend(): pl.pallas_call(kernel, out_shape=jax.ShapeDtypeStruct((ROWS, QROWS, HD),...]
where the time goes in v1:
time: 77.7 us; the launch traced here: 77.6 us
  Pallas kernels  74.9 us (96%)
  local copies, waits for them, and re-layouts  2.69 us (3%)
    pallas_call x1, Pallas kernels, attend(): pl.pallas_call(kernel, out_shape=jax.ShapeDtypeStruct((ROWS, QROWS, HD),...  74.9 us

profile of v1, /device:TPU:1, one launch (start us, length us, event | category | flops | bytes accessed | tf_op | source)
XLA Modules:
  0.0 77.6 jit_solution(15403237860813298561)
XLA Ops:
  0.0 0.0 copy-start
  0.0 0.9 %copy_bitcast_fusion.2 = (bf16[1,32,8,128]{3,1,0,2:T(8,128)(2,1)S(1)}, bf16[1,32,8,128]{3,1,0,2:T(8,128)(2,1)S(1)}) fusion(bf16[32,8,128]{2,1,0:T(8,128)(2,1)} %param.6, bf16[32,8,128]{2,1,0:T(8,128)(2,1)} %param.5), kind=kLoop, calls=%fused_computation.3 | loop fusion | bytes 262144 | tf_op jit(solution)/shard_map/stack | solution.py:412
  1.0 0.1 copy-done
  1.1 0.0 copy-start.1
  1.1 0.1 copy_bitcast_fusion.1.qs
  1.2 0.6 copy-done.1
  1.8 74.9 %attend.1 = bf16[8,256,128]{2,1,0:T(8,128)(2,1)S(1)} custom-call(bf16[8,256,128]{2,1,0:T(8,128)(2,1)S(1)} %copy_bitcast_fusion.1.qs, bf16[8,2,32,128]{3,2,1,0:T(8,128)(2,1)S(1)} %maximum_bitcast_fusion.kvs, s32[2,128]{1,0:T(2,128)S(1)} %bitcast.21), custom_call_target="tpu_custom_call" | custom-call | tf_op jit(solution)/shard_map/attend/pallas_call | solution.py:415
  76.6 0.9 %copy_bitcast_fusion = bf16[32,64,128]{2,1,0:T(8,128)(2,1)} fusion(bf16[8,256,128]{2,1,0:T(8,128)(2,1)S(1)} %attend.1), kind=kLoop, calls=%fused_computation | loop fusion | bytes 1048576 | tf_op jit(solution)/shard_map/reshape | solution.py:444
  (1 shorter events, 0.0 us)
Async XLA Ops:
  0.0 1.1 %copy-start = (bf16[32,64,128]{2,1,0:T(8,128)(2,1)S(1)}, bf16[32,64,128]{2,1,0:T(8,128)(2,1)}, u32[]{:S(2)}) copy-start(bf16[32,64,128]{2,1,0:T(8,128)(2,1)} %param.4) | copy-start | bytes 1572868
  1.1 0.7 copy-start.1

commit v2 on v1

--- a/solution.py
+++ b/solution.py
@@ -247,8 +247,7 @@
         high = r - jnp.where(zk < z, 0, 1)
         return jnp.maximum(high - spread, 0)
 
-    @pl.loop(0, ROWS)
-    def _(i):
+    def arrive(i):
         half = (i + 1) // 2
         d = (half + (i + 1) % 2 * (COLS - 2 * half)) % ROWS
 
@@ -260,32 +259,39 @@
         def _():
             qcopy(d).wait_recv()
 
-        r = (y + ROWS - d) % ROWS
-        r0 = base(r, z, 3)
-        q = jnp.concatenate([qbuf[r], jnp.where(lane < DOCS, qa[r], 0.0).astype(BF16)], axis=1)
-        k = jnp.concatenate([kvbuf[0, r, z].reshape(BLK, HD), kaug[z, r]], axis=1)
-        s = lax.dot_general(q, k, NT, preferred_element_type=F32)
+        return (y + ROWS - d) % ROWS
+
+    @pl.loop(0, ROWS // 2)
+    def _(pair):
+        parts = [arrive(2 * pair), arrive(2 * pair + 1)]
         at = (CS * TOK) * x + TOK * c + lax.broadcasted_iota(jnp.int32, (QROWS, BLK), 0) // PG
-        s = jnp.where(lax.broadcasted_iota(jnp.int32, (QROWS, BLK), 1) <= at, s, -BIG)
-        s1, s2 = s_tile(r, r0, z), s_tile(r, r0 + 2, z)
-        new = jnp.maximum(jnp.maximum(top_of(s), top_of(s1)), top_of(s2))
-        new = jnp.broadcast_to(new, (QROWS, HD))
-        top[r] = new
-        acc[r] = (
-            weigh(s, new, kvbuf[1, r, z].reshape(BLK, HD))
-            + weigh(s1, new, v_tile(r0, z))
-            + weigh(s2, new, v_tile(r0 + 2, z))
-        )
-
-        @pl.when(i == 1)
+        causal = lax.broadcasted_iota(jnp.int32, (QROWS, BLK), 1) <= at
+        scores = []
+        for r in parts:
+            q = jnp.concatenate([qbuf[r], jnp.where(lane < DOCS, qa[r], 0.0).astype(BF16)], axis=1)
+            k = jnp.concatenate([kvbuf[0, r, z].reshape(BLK, HD), kaug[z, r]], axis=1)
+            s = lax.dot_general(q, k, NT, preferred_element_type=F32)
+            r0 = base(r, z, 3)
+            scores.append((r, r0, jnp.where(causal, s, -BIG), s_tile(r, r0, z), s_tile(r, r0 + 2, z)))
+        for r, r0, s, s1, s2 in scores:
+            new = jnp.maximum(jnp.maximum(top_of(s), top_of(s1)), top_of(s2))
+            new = jnp.broadcast_to(new, (QROWS, HD))
+            top[r] = new
+            acc[r] = (
+                weigh(s, new, kvbuf[1, r, z].reshape(BLK, HD))
+                + weigh(s1, new, v_tile(r0, z))
+                + weigh(s2, new, v_tile(r0 + 2, z))
+            )
+
+        @pl.when(pair == 0)
         def _():
             k_event(1, (2, 3))
 
-        @pl.when(i == 3)
+        @pl.when(pair == 1)
         def _():
             v_event(3)
 
-        @pl.when(i == 5)
+        @pl.when(pair == 2)
         def _():
             pass_on(7)
 
@@ -364,20 +370,24 @@
 
     sbuf[0] = s_tile(*last_place(0))
 
-    @pl.loop(0, ROWS)
-    def _(i):
-        d = dist(i)
-        r = (y + d) % ROWS
-        for u in range(2 * len(LATE)):
-            f = 2 * len(LATE) * i + u
-            sbuf[(u + 1) % 2] = s_tile(*last_place(jnp.minimum(f + 1, 2 * len(LATE) * ROWS - 1)))
-            update(*last_place(f), sbuf[u % 2])
-        done = acc[r]
-        obuf[r] = (done[:, :HD] / done[:, HD:]).astype(BF16)
-
-        @pl.when(d > 0)
-        def _():
-            ocopy(d).start()
+    @pl.loop(0, ROWS // 2)
+    def _(pair):
+        for i, shift in ((2 * pair, 0), (2 * pair + 1, 2 * len(LATE))):
+            d = dist(i)
+            r = (y + d) % ROWS
+            for u in range(2 * len(LATE)):
+                f = 4 * len(LATE) * pair + shift + u
+                sbuf[(u + 1) % 2] = s_tile(*last_place(jnp.minimum(f + 1, 2 * len(LATE) * ROWS - 1)))
+                update(*last_place(f), sbuf[u % 2])
+            done = acc[r]
+            obuf[r] = (done[:, :HD] / done[:, HD:]).astype(BF16)
+            if shift == 0:
+                ocopy(d).start()
+            else:
+
+                @pl.when(d > 0)
+                def _():
+                    ocopy(d).start()
 
     own_o = pltpu.make_async_copy(obuf.at[y], o_ref.at[y], loc.at[2])
     own_o.start()

time: 77.7 us -> 77.4 us (level)
  no operation moved by 1% of the time
where the time goes in v2:
time: 77.4 us; the launch traced here: 77.2 us
  Pallas kernels  74.5 us (96%)
  local copies, waits for them, and re-layouts  2.69 us (3%)
    pallas_call x1, Pallas kernels, attend(): pl.pallas_call(kernel, out_shape=jax.ShapeDtypeStruct((ROWS, QROWS, HD),...  74.5 us

profile of v2, /device:TPU:1, one launch (start us, length us, event | category | flops | bytes accessed | tf_op | source)
XLA Modules:
  0.0 77.2 jit_solution(14193915507108163010)
XLA Ops:
  0.0 0.0 copy-start
  0.0 0.9 %copy_bitcast_fusion.2 = (bf16[1,32,8,128]{3,1,0,2:T(8,128)(2,1)S(1)}, bf16[1,32,8,128]{3,1,0,2:T(8,128)(2,1)S(1)}) fusion(bf16[32,8,128]{2,1,0:T(8,128)(2,1)} %param.6, bf16[32,8,128]{2,1,0:T(8,128)(2,1)} %param.5), kind=kLoop, calls=%fused_computation.3 | loop fusion | bytes 262144 | tf_op jit(solution)/shard_map/stack | solution.py:422
  1.0 0.1 copy-done
  1.1 0.0 copy-start.1
  1.1 0.1 copy_bitcast_fusion.1.qs
  1.2 0.6 copy-done.1
  1.8 74.5 %attend.1 = bf16[8,256,128]{2,1,0:T(8,128)(2,1)S(1)} custom-call(bf16[8,256,128]{2,1,0:T(8,128)(2,1)S(1)} %copy_bitcast_fusion.1.qs, bf16[8,2,32,128]{3,2,1,0:T(8,128)(2,1)S(1)} %maximum_bitcast_fusion.kvs, s32[2,128]{1,0:T(2,128)S(1)} %bitcast.21), custom_call_target="tpu_custom_call" | custom-call | tf_op jit(solution)/shard_map/attend/pallas_call | solution.py:425
  76.3 0.9 %copy_bitcast_fusion = bf16[32,64,128]{2,1,0:T(8,128)(2,1)} fusion(bf16[8,256,128]{2,1,0:T(8,128)(2,1)S(1)} %attend.1), kind=kLoop, calls=%fused_computation | loop fusion | bytes 1048576 | tf_op jit(solution)/shard_map/reshape | solution.py:454
  (1 shorter events, 0.0 us)
Async XLA Ops:
  0.0 1.1 %copy-start = (bf16[32,64,128]{2,1,0:T(8,128)(2,1)S(1)}, bf16[32,64,128]{2,1,0:T(8,128)(2,1)}, u32[]{:S(2)}) copy-start(bf16[32,64,128]{2,1,0:T(8,128)(2,1)} %param.4) | copy-start | bytes 1572868
  1.1 0.7 copy-start.1
